TPU v7x, 128 devices: a whole 4x4x4 slice. The times are simulated.
128 devices in a mesh: node: 8 (over x, core), local: 16 (over y, z).
Axes of the slice: x: 4, y: 4, z: 4, core: 2. Of those that a mesh axis runs over, the one named last changes fastest.
Arguments:
- tokens: bfloat16 [2048, 7168], P('local'), may hold values from -6 to 6
- expert_ids: int32 [2048, 8], P('local'), may hold values from 0 to 31, all different within a row; in each aligned block of 128 rows (0 to 127, 128 to 255, ...) at most 48 rows name the same one
- expert_scores: float32 [2048, 8], P('local'), may hold values from 0.05 to 1
- w_gate: bfloat16 [32, 7168, 2048], P('local', None, 'node'), may hold values from -0.0625 to 0.0625
- w_up: bfloat16 [32, 7168, 2048], P('local', None, 'node'), may hold values from -0.0625 to 0.0625
- w_down: bfloat16 [32, 2048, 7168], P('local', None, 'node'), may hold values from -0.125 to 0.125
Outputs:
- moe_output: bfloat16 [2048, 7168], P('local', 'node')
Inputs may be any that keep to these rules, and one draw needn't show every extreme that they name: `expert_ids`: each token names 8 different experts. Among the rows of one index of local no expert is named more than 48 times, and in every draw some index of local names some expert exactly 48 times.
All inputs are finite; a program needn't handle non-finite values.
Results may differ from a plain program's by a relative error of at most 0.012.
Values may be sent and summed in bfloat16 or wider, within the bound.
No kernel may reach another device: no remote copies, remote signals or barrier semaphores. Data moves between devices by JAX's collectives and lax.ppermute only.
A program may use at most 192 MiB of HBM per device.

v0:
```python
import jax
import jax.numpy as jnp
from jax import lax
from jax.sharding import PartitionSpec as P


def expand_hidden(rows, w_gate, w_up):
    gate = jnp.einsum("emcd,edf->emcf", rows, w_gate, preferred_element_type=jnp.float32)
    upper = jnp.einsum("emcd,edf->emcf", rows, w_up, preferred_element_type=jnp.float32)
    return (jax.nn.silu(gate) * upper).astype(jnp.bfloat16)


def body(tokens, expert_ids, expert_scores, w_gate, w_up, w_down):
    n_local = lax.axis_size("local")
    tok_rows, top_count = expert_ids.shape
    exp_local = w_gate.shape[0]
    experts_all = exp_local * n_local
    capacity = 3 * tok_rows * top_count // (2 * experts_all)
    highest = lax.Precision.HIGHEST
    flat_ids = expert_ids.reshape(-1)
    picked = (flat_ids[:, None] == jnp.arange(experts_all, dtype=jnp.int32)[None, :]).astype(
        jnp.int32
    )
    before = jnp.cumsum(picked, axis=0) - picked
    place = jnp.sum(before * picked, axis=1)
    slot_key = flat_ids * capacity + place
    slot_table = (
        slot_key[:, None] == jnp.arange(experts_all * capacity, dtype=jnp.int32)[None, :]
    ).astype(jnp.float32)
    slot_table = slot_table.reshape(tok_rows, top_count, n_local, exp_local, capacity)
    share = expert_scores / jnp.sum(expert_scores, axis=1, keepdims=True)
    dispatch_table = jnp.sum(slot_table, axis=1).astype(jnp.bfloat16)
    combine_table = jnp.einsum("tk,tklec->tlec", share, slot_table, precision=highest)
    weight_high = combine_table.astype(jnp.bfloat16)
    weight_low = (combine_table - weight_high.astype(jnp.float32)).astype(jnp.bfloat16)
    packed = jnp.einsum(
        "tlec,td->elcd", dispatch_table, tokens, preferred_element_type=jnp.float32
    ).astype(jnp.bfloat16)
    hidden = expand_hidden(
        lax.all_to_all(packed, "local", split_axis=1, concat_axis=1, tiled=True), w_gate, w_up
    )
    summed = jnp.einsum(
        "emcf,efj->emcj",
        lax.all_gather(hidden, "node", axis=3, tiled=True),
        w_down,
        preferred_element_type=jnp.float32,
    )
    expert_out = summed.astype(jnp.bfloat16)
    returned = lax.all_to_all(expert_out, "local", split_axis=1, concat_axis=1, tiled=True)
    mixed = jnp.einsum("tlec,elcj->tj", weight_high, returned, preferred_element_type=jnp.float32)
    mixed = mixed + jnp.einsum(
        "tlec,elcj->tj", weight_low, returned, preferred_element_type=jnp.float32
    )
    return mixed.astype(jnp.bfloat16)


def solution(mesh):
    placed = (
        P("local", None),
        P("local", None),
        P("local", None),
        P("local", None, "node"),
        P("local", None, "node"),
        P("local", None, "node"),
    )
    return jax.shard_map(
        body, mesh=mesh, in_specs=placed, out_specs=P("local", "node"), check_vma=False
    )
```

profile of v0, /device:TPU:0, one launch (start us, length us, event | category | flops | bytes accessed | tf_op | source)
XLA Modules:
  0.0 414.1 jit_solution(9511137174949946038)
XLA Ops:
  6.5 0.0 copy-start
  6.5 0.0 all-gather.2.cloned.1.call-start
  6.6 0.9 copy.39
  7.5 0.1 eq.56
  7.6 0.1 eq.52
  7.7 0.7 reduce_sum.29
  8.4 0.7 broadcast_divide_fusion
  9.1 9.0 %reduce-window.6 = s32[32,8,128]{2,1,0:T(8,128)S(1)} reduce-window(s32[32,8,128]{2,1,0:T(8,128)S(1)} %fusion.38, s32[]{:T(128)} %constant.15.clone.1), window={size=1x1x128 pad=0_0x0_0x127_0}, to_apply=%region_1.2 | reduce-window | flops 4161536 | bytes 262148 | tf_op jit(solution)/shard_map/reduce-window
  18.1 0.1 slice.8
  18.2 0.1 copy.41
  18.4 0.1 copy.42
  18.4 0.1 broadcast_add_fusion
  18.6 0.1 reduce_sum.31
  18.7 0.7 multiply_add_fusion.1
  19.4 1.3 fusion.8
  20.7 0.0 copy-done
  20.8 0.0 slice-start
  20.8 10.6 %convert_bitcast_fusion = bf16[2,16,48,7168]{3,2,0,1:T(8,128)(2,1)} fusion(bf16[128,7168]{1,0:T(8,128)(2,1)S(1)} %copy-done, bf16[128,16,2,48]{0,3,2,1:T(8,128)(2,1)S(1)} %get-tuple-element.6), kind=kOutput, calls=%fused_computation | convolution fusion | flops 2829582336 | bytes 24248320 | tf_op jit(solution)/shard_map/tlec,td->elcd/dot_general | solution.py:36
  31.3 253.1 %all_to_all.10 = bf16[2,16,48,7168]{3,2,0,1:T(8,128)(2,1)} all-to-all(bf16[2,16,48,7168]{3,2,0,1:T(8,128)(2,1)} %convert_bitcast_fusion), channel_id=1, replica_groups=mesh['node'=8,'local'=16] {'local'}, dimensions={1} | all-to-all | bytes 44040192 | tf_op jit(solution)/shard_map/all_to_all | solution.py:40
  284.5 0.0 slice-done
  284.5 0.0 slice-done.1
  284.5 10.3 %fusion.2 = f32[2,16,48,256]{3,2,1,0:T(8,128)S(1)} fusion(bf16[2,16,48,7168]{3,2,0,1:T(8,128)(2,1)} %all_to_all.10, bf16[2,7168,256]{2,1,0:T(8,128)(2,1)S(1)} %bitcast.61), kind=kOutput, calls=%fused_computation.3 | convolution fusion | flops 5637144576 | bytes 30932992 | tf_op jit(solution)/shard_map/emcd,edf->emcf/dot_general | solution.py:8
  294.8 13.2 %multiply_convert_fusion = bf16[2,16,48,256]{3,2,1,0:T(8,128)(2,1)} fusion(f32[2,16,48,256]{3,2,1,0:T(8,128)S(1)} %fusion.2, bf16[2,7168,256]{2,1,0:T(8,128)(2,1)} %param.10, bf16[2,16,48,7168]{3,2,0,1:T(8,128)(2,1)} %all_to_all.10), kind=kOutput, calls=%fused_computation.19 | convolution fusion | flops 5639503872 | bytes 31719424 | tf_op jit(solution)/shard_map/emcd,edf->emcf/dot_general | solution.py:9
  308.0 0.0 all-gather.2.cloned.1.call-update
  308.0 43.7 %all-gather.2.cloned.1.call-done = bf16[2,16,48,2048]{3,2,1,0:T(8,128)(2,1)} async-done(((bf16[2,16,48,256]{3,2,1,0:T(8,128)(2,1)}), bf16[2,16,48,2048]{3,2,1,0:T(8,128)(2,1)}) %all-gather.2.cloned.1.call-update) | async-done | bytes 6291472 | tf_op jit(solution)/shard_map/all_gather | solution.py:44
  351.7 10.9 %fusion.14 = bf16[2,16,48,896]{3,2,1,0:T(8,128)(2,1)S(1)} fusion(bf16[2,16,48,2048]{3,2,1,0:T(8,128)(2,1)} %all-gather.2.cloned.1.call-done, bf16[2,2048,896]{2,1,0:T(8,128)(2,1)} %param.11), kind=kOutput, calls=%fused_computation.17 | convolution fusion | flops 5638520832 | bytes 16384000 | tf_op jit(solution)/shard_map/emcf,efj->emcj/dot_general | solution.py:42
  362.6 0.0 copy-start.1
  362.6 0.2 copy.46
  362.8 42.6 %all_to_all.11 = bf16[2,16,48,896]{3,2,0,1:T(8,128)(2,1)S(1)} all-to-all(bf16[2,16,48,896]{3,2,0,1:T(8,128)(2,1)S(1)} %copy.46), channel_id=1, replica_groups=mesh['node'=8,'local'=16] {'local'}, dimensions={1} | all-to-all | bytes 5505024 | tf_op jit(solution)/shard_map/all_to_all | solution.py:49
  405.4 0.6 fusion.22
  406.0 1.3 fusion.31
  407.3 0.0 copy-done.1
  (8 shorter events, 0.1 us)
Async XLA Ops:
  6.5 14.2 %copy-start = (bf16[128,7168]{1,0:T(8,128)(2,1)S(1)}, bf16[128,7168]{1,0:T(8,128)(2,1)}, u32[]{:S(2)}) copy-start(bf16[128,7168]{1,0:T(8,128)(2,1)} %param.6) | copy-start | bytes 5505028
  6.5 345.1 %all-gather.2.cloned.1.call-start = ((), (), s32[]{:S(2)}) async-start(), calls=%async_computation.2 | async-start | bytes 7077888 | tf_op jit(solution)/shard_map/all_gather | solution.py:44
  20.8 263.7 %slice-start = ((s8[7340032]{0:T(1024)(128)(4,1)}), s8[3145728]{0:T(1024)(128)(4,1)S(1)}, s32[]{:S(2)}) async-start(s8[7340032]{0:T(1024)(128)(4,1)} %bitcast.60), calls=%async_computation.3 | async-start | bytes 6291456
  31.3 253.1 %slice-start.1 = ((s8[7340032]{0:T(1024)(128)(4,1)}), s8[4194304]{0:T(1024)(128)(4,1)S(1)}, s32[]{:S(2)}) async-start(s8[7340032]{0:T(1024)(128)(4,1)} %bitcast.60), calls=%async_computation.4 | async-start | bytes 8388608
  362.6 44.7 %copy-start.1 = (bf16[128,7168]{1,0:T(8,128)(2,1)S(1)}, bf16[128,7168]{1,0:T(8,128)(2,1)}, u32[]{:S(2)}) copy-start(bf16[128,7168]{1,0:T(8,128)(2,1)} %param.6) | copy-start | bytes 5505028
Sparse Core Ops, SparseCore 0:
  308.1 43.5 all-gather.1
where the time goes:
time: 414 us
  blocking collectives  296 us (71%)
  matrix products  46.9 us (11%)
  waiting for transfers between devices  43.7 us (11%)
  between operations  13.5 us (3%)
  other arithmetic  12.6 us (3%)
    all_to_all x1, blocking collectives, body(): lax.all_to_all(packed, 'local', split_axis=1, concat_axis=1, tiled=True)  253 us
    all_gather x1, waiting for transfers between devices, body(): lax.all_gather(hidden, 'node', axis=3, tiled=True)  43.7 us
    all_to_all x1, blocking collectives, body(): lax.all_to_all(expert_out, 'local', split_axis=1, concat_axis=1, tiled=True)  42.6 us
    dot_general x1, matrix products, expand_hidden(): jnp.einsum('emcd,edf->emcf', rows, w_up, preferred_element_type=jnp.float32)  13.2 us
    dot_general x1, matrix products, body(): jnp.einsum('emcf,efj->emcj', lax.all_gather(hidden, 'node', axis=3, tiled...  10.9 us
    dot_general x1, matrix products, body(): jnp.einsum('tlec,td->elcd', dispatch_table, tokens, preferred_element_typ...  10.6 us
    dot_general x1, matrix products, expand_hidden(): jnp.einsum('emcd,edf->emcf', rows, w_gate, preferred_element_type=jnp.flo...  10.3 us
    another operation x3, other arithmetic  9.15 us
  transfers between devices with their start and end apart: 1, of which 1 were waited for; matrix products, arithmetic and copies ran while one was open for 0% of the time, Pallas kernels for 0%

commit v1 on v0

v1 whole, which is shorter than its diff:
```python
import functools

import jax
import jax.numpy as jnp
from jax import lax
from jax.experimental import pallas as pl
from jax.experimental.pallas import tpu as pltpu
from jax.sharding import PartitionSpec as P

BF = jnp.bfloat16
F32 = jnp.float32
AXES = ("node", "local")
SIDE = 4
CAP = 48
META = 128
STEP = 896
VMEM_LIMIT = 56 * 2**20
CHUNKS = (
    ((0, 0), (1, 1), (3, 3), (0, 3), (3, 0)),
    ((2, 2), (2, 0), (0, 2), (2, 1), (1, 2)),
    ((3, 1), (2, 3), (1, 3), (3, 2), (0, 1), (1, 0)),
)


def device_at(x, c, y, z):
    return (x * 2 + c) * 16 + y * 4 + z


def hop(value, dx=0, dc=0, dy=0, dz=0):
    pairs = [
        (device_at(x, c, y, z), device_at((x + dx) % 4, (c + dc) % 2, (y + dy) % 4, (z + dz) % 4))
        for x in range(4)
        for c in range(2)
        for y in range(4)
        for z in range(4)
    ]
    return lax.ppermute(value, AXES, pairs)


def spread_first(own, first):
    own = own[None]
    return {
        0: own,
        1: hop(own, **{first: -1}),
        3: hop(own, **{first: 1}),
        2: hop(own, **{first: 2}),
    }


def spread_second(near, second):
    pair = {"l": jnp.concatenate([near[1], near[2]]), "r": jnp.concatenate([near[3], near[0]])}
    l_1 = hop(pair["l"], **{second: -1})
    r_3 = hop(pair["r"], **{second: 1})
    l_2 = hop(l_1, **{second: -1})
    r_2 = hop(r_3, **{second: 1})
    r_1 = hop(pair["r"], **{second: -1})
    l_3 = hop(pair["l"], **{second: 1})
    found = {(d, 0): (near[d], 0) for d in range(4)}
    for e, left, right in ((1, l_1, r_1), (3, l_3, r_3), (2, l_2, r_2)):
        found[1, e], found[2, e] = (left, 0), (left, 1)
        found[3, e], found[0, e] = (right, 0), (right, 1)
    return found


def expand_kernel(count, halves, _, *refs):
    blocks_a, blocks_b = refs[:count], refs[count : 2 * count]
    table, *weights = refs[2 * count : 2 * count + 5]
    own, other, rows, total = refs[2 * count + 5 :]
    k = pl.program_id(0)

    def pick(blocks):
        for s in range(count):
            picked = jnp.dot(table[s], blocks[s][0], preferred_element_type=F32).astype(BF)
            for e in range(2):
                rows[e, s * CAP : (s + 1) * CAP, :] = picked[e * CAP : (e + 1) * CAP]

    @pl.when(k < halves)
    def _():
        pick(blocks_a)

    @pl.when(k >= halves)
    def _():
        pick(blocks_b)

    @pl.when(k == 0)
    def _():
        total[...] = jnp.zeros_like(total)

    for e in range(2):
        for n, weight in enumerate(weights):
            at = slice(n * weight.shape[2], (n + 1) * weight.shape[2])
            total[e, :, at] += jnp.dot(rows[e], weight[e], preferred_element_type=F32)

    @pl.when(k == 2 * halves - 1)
    def _():
        split = own.shape[2]
        own[...] = total[:, :, :split]
        other[...] = total[:, :, split:].astype(BF)


def expand(core, sources_a, sources_b, table, own_weights, other_weights):
    count = len(sources_a)
    units = own_weights[0].shape[2]
    rows = count * CAP
    half = other_weights[0].shape[1]
    halves = half // 2 // STEP

    def part_a(index):
        return pl.BlockSpec((1, 128, STEP), lambda k, c: (index, 0, jnp.minimum(k, halves - 1)))

    def part_b(index):
        return pl.BlockSpec((1, 128, STEP), lambda k, c: (index, 0, jnp.maximum(k - halves, 0)))

    result = pl.BlockSpec((2, rows, 2 * units), lambda k, c: (0, 0, 0))
    own_spec = pl.BlockSpec((2, STEP, units), lambda k, c: (0, c[0] * 2 * halves + k, 0))
    other_spec = pl.BlockSpec((2, STEP, units), lambda k, c: (0, k, 0))
    return pl.pallas_call(
        functools.partial(expand_kernel, count, halves),
        grid_spec=pltpu.PrefetchScalarGridSpec(
            num_scalar_prefetch=1,
            grid=(2 * halves,),
            in_specs=[part_a(i) for _, i in sources_a]
            + [part_b(i) for _, i in sources_b]
            + [pl.BlockSpec(table.shape, lambda k, c: (0, 0, 0))]
            + [own_spec] * 2
            + [other_spec] * 2,
            out_specs=[result, result],
            scratch_shapes=[
                pltpu.VMEM((2, rows, STEP), BF),
                pltpu.VMEM((2, rows, 4 * units), F32),
            ],
        ),
        out_shape=[
            jax.ShapeDtypeStruct((2, rows, 2 * units), F32),
            jax.ShapeDtypeStruct((2, rows, 2 * units), BF),
        ],
        compiler_params=pltpu.CompilerParams(vmem_limit_bytes=VMEM_LIMIT),
        cost_estimate=pl.CostEstimate(
            flops=16 * rows * half * units + 4 * rows * 128 * half,
            bytes_accessed=count * 256 * half + 16 * half * units + 24 * rows * units,
            transcendentals=0,
        ),
    )(
        core,
        *[a for a, _ in sources_a],
        *[a for a, _ in sources_b],
        table,
        *own_weights,
        *other_weights,
    )


def contract_kernel(count, pieces, stacked, blocks, *refs):
    hidden, (weight, table), outs = refs[:stacked], refs[stacked : stacked + 2], refs[stacked + 2 :]
    depth = hidden[0].shape[-1]
    results = []
    for e in range(2):
        total = None
        for p in range(pieces):
            value = hidden[0][p, e] if stacked == 1 else hidden[p][e]
            start = pl.multiple_of(blocks[p] * depth, depth)
            part = jnp.dot(value, weight[e, pl.ds(start, depth), :], preferred_element_type=F32)
            total = part if total is None else total + part
        results.append(total.astype(BF))
    for s in range(count):
        rows = jnp.concatenate([r[s * CAP : (s + 1) * CAP] for r in results])
        outs[s][...] = jnp.dot(table[s], rows, preferred_element_type=F32).astype(BF)


def contract(blocks, hidden, weight, table):
    count, tokens, _ = table.shape
    pieces = blocks.shape[0]
    rows = count * CAP
    width = weight.shape[2]
    in_vmem = pl.BlockSpec(memory_space=pltpu.VMEM)
    return pl.pallas_call(
        functools.partial(contract_kernel, count, pieces, len(hidden)),
        in_specs=[pl.BlockSpec(memory_space=pltpu.SMEM)] + [in_vmem] * (len(hidden) + 2),
        out_specs=[in_vmem] * count,
        out_shape=[jax.ShapeDtypeStruct((tokens, width), BF)] * count,
        compiler_params=pltpu.CompilerParams(vmem_limit_bytes=VMEM_LIMIT),
        cost_estimate=pl.CostEstimate(
            flops=4 * rows * weight.shape[1] * width + 4 * rows * tokens * width,
            bytes_accessed=4 * rows * weight.shape[1]
            + 4 * weight.shape[1] * width
            + count * tokens * width * 2,
            transcendentals=0,
        ),
    )(blocks, *hidden, weight, table)


def tables(meta, place):
    top = 8
    ids = meta[..., :top]
    shares = meta[..., top : 2 * top] + meta[..., 2 * top : 3 * top]
    count, tokens, _ = ids.shape
    wanted = (place * 2 + jnp.arange(2)).astype(F32)
    hit = ids[:, None] == wanted[None, :, None, None]
    picked = jnp.any(hit, axis=-1)
    weigh = jnp.sum(jnp.where(hit, shares[:, None], 0.0), axis=-1)
    earlier = jnp.tril(jnp.ones((tokens, tokens), BF), -1)
    rank = jnp.einsum("set,ut->seu", picked.astype(BF), earlier, preferred_element_type=F32)
    chosen = jnp.where(picked, rank, -1.0)
    slot = chosen[:, :, None, :] == jnp.arange(CAP, dtype=F32)[None, None, :, None]
    row_share = jnp.sum(jnp.where(slot, weigh[:, :, None, :], 0.0), axis=-1)
    gather_table = slot.astype(BF).reshape(count, 2 * CAP, tokens)
    combine_table = (
        (chosen[:, :, :, None] == jnp.arange(CAP, dtype=F32)).astype(BF).transpose(0, 2, 1, 3)
    ).reshape(count, tokens, 2 * CAP)
    scale = row_share.transpose(1, 0, 2).reshape(2, count * CAP, 1)
    return gather_table, combine_table, scale


def body(tokens, expert_ids, expert_scores, w_gate, w_up, w_down):
    width = tokens.shape[1]
    half = width // 2
    part = half // 2
    units = w_gate.shape[2]
    node, place = lax.axis_index("node"), lax.axis_index("local")
    x, c = node // 2, node % 2
    core = c.astype(jnp.int32).reshape(1)

    share = expert_scores / jnp.sum(expert_scores, axis=1, keepdims=True)
    high = share.astype(BF)
    low = (share - high.astype(F32)).astype(BF)
    meta = jnp.concatenate([expert_ids.astype(BF), high, low], axis=1)
    meta = jnp.pad(meta, ((0, 0), (0, META - meta.shape[1])))

    mine_a = lax.dynamic_slice_in_dim(tokens, c * half, part, axis=1)
    mine_b = lax.dynamic_slice_in_dim(tokens, c * half + part, part, axis=1)
    near_a = spread_first(jnp.concatenate([mine_a, meta], axis=1), "dy")
    near_b = spread_first(mine_b, "dz")

    gate_w, up_w, near_a[1], near_b[1] = lax.optimization_barrier(
        (w_gate, w_up, near_a[1], near_b[1])
    )
    other_gate = hop(lax.dynamic_slice_in_dim(gate_w, (1 - c) * half, half, axis=1), dc=1)
    other_up = hop(lax.dynamic_slice_in_dim(up_w, (1 - c) * half, half, axis=1), dc=1)

    found_a = spread_second(near_a, "dz")
    found_b = spread_second(near_b, "dy")

    blocks_abs = jnp.arange(8, dtype=jnp.int32)
    blocks_rel = jnp.stack(
        [
            ((x + dx) % 4) * 2 + (c + dc) % 2
            for dx, dc in ((0, 0), (3, 0), (1, 0), (2, 0), (0, 1), (3, 1), (1, 1), (2, 1))
        ]
    ).astype(jnp.int32)

    final = None
    for number, chunk in enumerate(CHUNKS):
        sources_a = [found_a[dy, dz] for dy, dz in chunk]
        sources_b = [found_b[dz, dy] for dy, dz in chunk]
        metas = jnp.stack([a[i, :, part : part + 24] for a, i in sources_a]).astype(F32)
        gather_table, combine_table, scale = tables(metas, place)
        total, away = expand(
            core, sources_a, sources_b, gather_table, (w_gate, w_up), (other_gate, other_up)
        )
        total = total + hop(away, dc=1).astype(F32)
        gate, upper = total[..., :units], total[..., units:]
        hidden = (jax.nn.silu(gate) * upper * scale).astype(BF)
        if number < len(CHUNKS) - 1:
            pieces = [lax.all_gather(hidden, "node", axis=0)]
            outs = contract(blocks_abs, pieces, w_down, combine_table)
        else:
            plane = [hidden, hop(hidden, dx=1), hop(hidden, dx=-1), hop(hidden, dx=2)]
            pieces = plane + [hop(p, dc=1) for p in plane]
            outs = contract(blocks_rel, pieces, w_down, combine_table)
        for (dy, dz), out in zip(chunk, outs):
            arrived = out if (dy, dz) == (0, 0) else hop(out, dy=dy, dz=dz)
            arrived = arrived.astype(F32)
            final = arrived if final is None else final + arrived
    return final.astype(BF)


def solution(mesh):
    placed = (
        P("local", None),
        P("local", None),
        P("local", None),
        P("local", None, "node"),
        P("local", None, "node"),
        P("local", None, "node"),
    )
    return jax.shard_map(
        body, mesh=mesh, in_specs=placed, out_specs=P("local", "node"), check_vma=False
    )
```

time: 414 us -> 320 us (0.77)
  blocking collectives: 296 us -> 0 us
  waiting for transfers between devices: 43.7 us -> 132 us
  starting transfers between devices: 0.01 us -> 63.8 us
  Pallas kernels: 0 us -> 57.9 us
  matrix products: 46.9 us -> 1.75 us
  local copies, waits for them, and re-layouts: 1.77 us -> 29.8 us
  other arithmetic: 12.6 us -> 18.6 us
    all_to_all x2 -> x0, blocking collectives: 296 us -> none  [the longest x1 253 us: body(): lax.all_to_all(packed, 'local', split_axis=1, concat_axis=1, tiled=True)]
    ppermute x0 -> x45, waiting for transfers between devices: none -> 132 us  [hop(): return lax.ppermute(value, AXES, pairs)]
    ppermute x0 -> x45, starting transfers between devices: none -> 63.8 us  [hop(): return lax.ppermute(value, AXES, pairs)]
    pallas_call x0 -> x6, Pallas kernels: none -> 57.9 us  [the longest x3 36.2 us: expand(): pl.pallas_call(functools.partial(expand_kernel, count, halves), grid_spec...]
    dot_general x6 -> x3, matrix products: 46.9 us -> 1.75 us  [tables(): jnp.einsum('set,ut->seu', picked.astype(BF), earlier, preferred_element_t...]
    all_gather x1 -> x2, waiting for transfers between devices: 43.7 us -> 0.01 us  [body(): pieces = [lax.all_gather(hidden, 'node', axis=0)]]
    convert_element_type x1 -> x14, other arithmetic: 0.01 us -> 9.53 us  [the longest x2 2.25 us: tables(): gather_table = slot.astype(BF).reshape(count, 2 * CAP, tokens)]
    another operation x3 -> x0, other arithmetic: 9.15 us -> none
  transfers between devices with their start and end apart: 1 -> 47, of which waited for: 1 -> 22; matrix products, arithmetic and copies ran while one was open for 0% -> 13% of each run, Pallas kernels for 0% -> 15%
where the time goes in v1:
time: 320 us; the launch traced here: 318 us
  waiting for transfers between devices  132 us (41%)
  starting transfers between devices  63.8 us (20%)
  Pallas kernels  57.9 us (18%)
  local copies, waits for them, and re-layouts  29.8 us (9%)
  other arithmetic  18.6 us (6%)
  between operations  14 us (4%)
    ppermute x45, waiting for transfers between devices, hop(): return lax.ppermute(value, AXES, pairs)  132 us
    ppermute x45, starting transfers between devices, hop(): return lax.ppermute(value, AXES, pairs)  63.8 us
    pallas_call x3, Pallas kernels, expand(): pl.pallas_call(functools.partial(expand_kernel, count, halves), grid_spec...  36.2 us
    pallas_call x3, Pallas kernels, contract(): pl.pallas_call(functools.partial(contract_kernel, count, pieces, len(hidd...  21.7 us
    unnamed x73, local copies, waits for them, and re-layouts  9.59 us
    slice x26, local copies, waits for them, and re-layouts, body(): a[i, :, part:part + 24]  6.57 us
  transfers between devices with their start and end apart: 47, of which 22 were waited for; matrix products, arithmetic and copies ran while one was open for 13% of the time, Pallas kernels for 15%

profile of v1, /device:TPU:0, one launch (start us, length us, event | category | flops | bytes accessed | tf_op | source)
XLA Modules:
  0.0 318.2 jit_solution(13975967223257195900)
XLA Ops:
  10.1 3.2 collective-permute-start
  13.2 4.0 %collective-permute-start.1 = (bf16[1,128,1792]{2,1,0:T(8,128)(2,1)S(1)}, bf16[1,128,1792]{2,1,0:T(8,128)(2,1)S(1)}, u32[]{:S(2)}, u32[]{:S(2)}) collective-permute-start(bf16[1,128,1792]{2,1,0:T(8,128)(2,1)S(1)} %get-tuple-element.61.refs_5_), channel_id=1, source_target_pairs={{0,3},{1,0},{2,1},{3,2},{4,7},{5,4},{6,5},{7,6},{8,11},{9,8},{10,9... | collective-permute-start | bytes 1376264 | tf_op jit(solution)/shard_map/ppermute | solution.py:37
  18.9 7.9 %collective-permute-done.1.refs_10_ = bf16[1,128,1792]{2,1,0:T(8,128)(2,1)S(1)} collective-permute-done((bf16[1,128,1792]{2,1,0:T(8,128)(2,1)S(1)}, bf16[1,128,1792]{2,1,0:T(8,128)(2,1)S(1)}, u32[]{:S(2)}, u32[]{:S(2)}) %collective-permute-start.1) | collective-permute-done | bytes 458784 | tf_op jit(solution)/shard_map/ppermute | solution.py:37
  26.8 7.5 %collective-permute-done.refs_5_ = bf16[1,128,1920]{2,1,0:T(8,128)(2,1)S(1)} collective-permute-done((bf16[1,128,1920]{2,1,0:T(8,128)(2,1)S(1)}, bf16[1,128,1920]{2,1,0:T(8,128)(2,1)S(1)}, u32[]{:S(2)}, u32[]{:S(2)}) %collective-permute-start) | collective-permute-done | bytes 491552 | tf_op jit(solution)/shard_map/ppermute | solution.py:37
  34.2 4.3 %constant_dynamic-slice_fusion.1 = bf16[2,3584,256]{2,1,0:T(8,128)(2,1)} fusion(bf16[2,7168,256]{2,1,0:T(8,128)(2,1)} %refs_13_.1, s32[]{:T(128)S(6)} %select_n.125), kind=kLoop, calls=%fused_computation.86 | loop fusion | bytes 7340036 | tf_op jit(solution)/shard_map/dynamic_slice | solution.py:237
  43.5 4.0 %collective-permute-start.3 = (bf16[2,128,1920]{2,1,0:T(8,128)(2,1)}, bf16[2,128,1920]{2,1,0:T(8,128)(2,1)S(1)}, u32[]{:S(2)}, u32[]{:S(2)}) collective-permute-start(bf16[2,128,1920]{2,1,0:T(8,128)(2,1)} %constant_dynamic-update-slice_fusion), channel_id=1, source_target_pairs={{0,3},{1,0},{2,1},{3,2},{4,7},{5,4},{6,5},{7,6},{8,11},{9,8},{10,9... | collective-permute-start | bytes 2949128 | tf_op jit(solution)/shard_map/ppermute | solution.py:37
  50.4 32.9 %collective-permute-done.8.refs_8_ = bf16[1,128,1792]{2,1,0:T(8,128)(2,1)S(1)} collective-permute-done((bf16[1,128,1792]{2,1,0:T(8,128)(2,1)S(1)}, bf16[1,128,1792]{2,1,0:T(8,128)(2,1)S(1)}, u32[]{:S(2)}, u32[]{:S(2)}) %collective-permute-start.8) | collective-permute-done | bytes 458784 | tf_op jit(solution)/shard_map/ppermute | solution.py:37
  87.2 9.0 %collective-permute-done.6.refs_7_ = bf16[1,128,1792]{2,1,0:T(8,128)(2,1)S(1)} collective-permute-done((bf16[1,128,1792]{2,1,0:T(8,128)(2,1)S(1)}, bf16[1,128,1792]{2,1,0:T(8,128)(2,1)S(1)}, u32[]{:S(2)}, u32[]{:S(2)}) %collective-permute-start.6) | collective-permute-done | bytes 458784 | tf_op jit(solution)/shard_map/ppermute | solution.py:37
  101.2 12.9 %collective-permute-done.17.refs_0_.refs_4_ = bf16[2,128,1920]{2,1,0:T(8,128)(2,1)S(1)} collective-permute-done((bf16[2,128,1920]{2,1,0:T(8,128)(2,1)S(1)}, bf16[2,128,1920]{2,1,0:T(8,128)(2,1)S(1)}, u32[]{:S(2)}, u32[]{:S(2)}) %collective-permute-start.17) | collective-permute-done | bytes 983072 | tf_op jit(solution)/shard_map/ppermute | solution.py:37
  114.1 3.7 %collective-permute-start.7 = (bf16[2,128,1792]{2,1,0:T(8,128)(2,1)}, bf16[2,128,1792]{2,1,0:T(8,128)(2,1)}, u32[]{:S(2)}, u32[]{:S(2)}) collective-permute-start(bf16[2,128,1792]{2,1,0:T(8,128)(2,1)} %copy-done.22), channel_id=1, source_target_pairs={{0,12},{1,13},{2,14},{3,15},{4,0},{5,1},{6,2},{7,3},{8,4},{9,5},{1... | collective-permute-start | bytes 2752520 | tf_op jit(solution)/shard_map/ppermute | solution.py:37
  131.4 5.4 %collective-permute-done.7.refs_6_.refs_9_ = bf16[2,128,1792]{2,1,0:T(8,128)(2,1)} collective-permute-done((bf16[2,128,1792]{2,1,0:T(8,128)(2,1)}, bf16[2,128,1792]{2,1,0:T(8,128)(2,1)}, u32[]{:S(2)}, u32[]{:S(2)}) %collective-permute-start.7) | collective-permute-done | bytes 917536 | tf_op jit(solution)/shard_map/ppermute | solution.py:37
  136.8 11.7 %shard_map.64 = (f32[2,240,512]{2,1,0:T(8,128)}, bf16[2,240,512]{2,1,0:T(8,128)(2,1)}) custom-call(s32[1]{0:T(128)} %bitcast._, bf16[1,128,1920]{2,1,0:T(8,128)(2,1)} %copy-done.1, bf16[2,128,1920]{2,1,0:T(8,128)(2,1)} %copy-done.3, bf16[2,128,1920]{2,1,0:T(8,128)(2,1)} %collective-permute-done.5.refs_2_.refs_3_, ...), custom_call_target="tpu_custom_call" | custom-call | flops 3963617280 | bytes 20742144 | tf_op jit(solution)/shard_map/pallas_call | solution.py:117
  153.1 3.6 %collective-permute-start.28 = (bf16[2,128,1920]{2,1,0:T(8,128)(2,1)}, bf16[2,128,1920]{2,1,0:T(8,128)(2,1)S(1)}, u32[]{:S(2)}, u32[]{:S(2)}) collective-permute-start(bf16[2,128,1920]{2,1,0:T(8,128)(2,1)} %constant_dynamic-update-slice_fusion), channel_id=1, source_target_pairs={{0,1},{1,2},{2,3},{3,0},{4,5},{5,6},{6,7},{7,4},{8,9},{9,10},{10,1... | collective-permute-start | bytes 2949128 | tf_op jit(solution)/shard_map/ppermute | solution.py:37
  156.7 3.7 %collective-permute-start.19 = (bf16[2,128,1792]{2,1,0:T(8,128)(2,1)}, bf16[2,128,1792]{2,1,0:T(8,128)(2,1)}, u32[]{:S(2)}, u32[]{:S(2)}) collective-permute-start(bf16[2,128,1792]{2,1,0:T(8,128)(2,1)} %collective-permute-done.7.refs_6_.refs_9_), channel_id=1, source_target_pairs={{0,12},{1,13},{2,14},{3,15},{4,0},{5,1},{6,2},{7,3},{8,4},{9,5},{1... | collective-permute-start | bytes 2752520 | tf_op jit(solution)/shard_map/ppermute | solution.py:37
  162.7 16.4 %collective-permute-done.28.refs_1_.refs_2_ = bf16[2,128,1920]{2,1,0:T(8,128)(2,1)S(1)} collective-permute-done((bf16[2,128,1920]{2,1,0:T(8,128)(2,1)}, bf16[2,128,1920]{2,1,0:T(8,128)(2,1)S(1)}, u32[]{:S(2)}, u32[]{:S(2)}) %collective-permute-start.28) | collective-permute-done | bytes 983072 | tf_op jit(solution)/shard_map/ppermute | solution.py:37
  181.9 11.6 %shard_map.66 = (f32[2,240,512]{2,1,0:T(8,128)}, bf16[2,240,512]{2,1,0:T(8,128)(2,1)}) custom-call(s32[1]{0:T(128)} %bitcast._, bf16[2,128,1920]{2,1,0:T(8,128)(2,1)} %copy-done.4, bf16[1,128,1920]{2,1,0:T(8,128)(2,1)} %copy-done.11, bf16[2,128,1920]{2,1,0:T(8,128)(2,1)} %copy-done.2, bf16[2,128,1920]{2,1,0:T(8,128)(2,1)} %copy-done.3, ...), custom_call_target="tpu_custom_call" | custom-call | flops 3963617280 | bytes 20742144 | tf_op jit(solution)/shard_map/pallas_call | solution.py:117
  200.0 3.4 %collective-permute-done.29.refs_6_.refs_9_ = bf16[2,128,1792]{2,1,0:T(8,128)(2,1)} collective-permute-done((bf16[2,128,1792]{2,1,0:T(8,128)(2,1)}, bf16[2,128,1792]{2,1,0:T(8,128)(2,1)}, u32[]{:S(2)}, u32[]{:S(2)}) %collective-permute-start.29) | collective-permute-done | bytes 917536 | tf_op jit(solution)/shard_map/ppermute | solution.py:37
  203.4 12.8 %shard_map.68 = (f32[2,288,512]{2,1,0:T(8,128)}, bf16[2,288,512]{2,1,0:T(8,128)(2,1)}) custom-call(s32[1]{0:T(128)} %bitcast._, bf16[2,128,1920]{2,1,0:T(8,128)(2,1)} %copy-done.6, bf16[2,128,1920]{2,1,0:T(8,128)(2,1)} %copy-done.5, bf16[2,128,1920]{2,1,0:T(8,128)(2,1)} %copy-done.5, bf16[2,128,1920]{2,1,0:T(8,128)(2,1)} %copy-done.2, ...), custom_call_target="tpu_custom_call" | custom-call | flops 4756340736 | bytes 21954560 | tf_op jit(solution)/shard_map/pallas_call | solution.py:117
  225.2 5.2 %collective-permute-done.32.refs_1_ = bf16[2,288,256]{2,1,0:T(8,128)(2,1)S(1)} collective-permute-done((bf16[2,288,256]{2,1,0:T(8,128)(2,1)S(1)}, bf16[2,288,256]{2,1,0:T(8,128)(2,1)S(1)}, u32[]{:S(2)}, u32[]{:S(2)}) %collective-permute-start.32) | collective-permute-done | bytes 294944 | tf_op jit(solution)/shard_map/ppermute | solution.py:37
  230.5 5.6 %collective-permute-done.33.refs_2_ = bf16[2,288,256]{2,1,0:T(8,128)(2,1)S(1)} collective-permute-done((bf16[2,288,256]{2,1,0:T(8,128)(2,1)S(1)}, bf16[2,288,256]{2,1,0:T(8,128)(2,1)S(1)}, u32[]{:S(2)}, u32[]{:S(2)}) %collective-permute-start.33) | collective-permute-done | bytes 294944 | tf_op jit(solution)/shard_map/ppermute | solution.py:37
  240.6 7.6 %shard_map.69 = (bf16[128,896]{1,0:T(8,128)(2,1)}, bf16[128,896]{1,0:T(8,128)(2,1)}, bf16[128,896]{1,0:T(8,128)(2,1)}, bf16[128,896]{1,0:T(8,128)(2,1)}, bf16[12...) custom-call(s32[8]{0:T(128)} %stack.47.blocks, bf16[2,288,256]{2,1,0:T(8,128)(2,1)} %copy-done.15, ...), custom_call_target="tpu_custom_call" | custom-call | flops 2246049792 | bytes 11075584 | tf_op jit(solution)/shard_map/pallas_call | solution.py:176
  248.3 2.5 collective-permute-start.39
  253.0 2.6 collective-permute-start.42
  257.3 7.1 %shard_map.65 = (bf16[128,896]{1,0:T(8,128)(2,1)}, bf16[128,896]{1,0:T(8,128)(2,1)}, bf16[128,896]{1,0:T(8,128)(2,1)}, bf16[128,896]{1,0:T(8,128)(2,1)}, bf16[128,896]{1,0:T(8,128)(2,1)}) custom-call(s32[8]{0:T(128)} %iota.65.blocks, bf16[8,2,240,256]{3,2,1,0:T(8,128)(2,1)} %bitcast.41, bf16[2,2048,896]{2,1,0:T(8,128)(2,1)} %refs_8_.1, ...), custom_call_target="tpu_custom_call" | custom-call | flops 1871708160 | bytes 10452992 | tf_op jit(solution)/shard_map/pallas_call | solution.py:176
  265.6 2.7 collective-permute-start.13
  268.4 6.6 %collective-permute-start.14 = (bf16[128,896]{1,0:T(8,128)(2,1)}, bf16[128,896]{1,0:T(8,128)(2,1)S(1)}, u32[]{:S(2)}, u32[]{:S(2)}) collective-permute-start(bf16[128,896]{1,0:T(8,128)(2,1)} %get-tuple-element.39), channel_id=1, source_target_pairs={{0,15},{1,12},{2,13},{3,14},{4,3},{5,0},{6,1},{7,2},{8,7},{9,4},{1... | collective-permute-start | bytes 688136 | tf_op jit(solution)/shard_map/ppermute | solution.py:37
  275.2 2.2 collective-permute-start.16
  277.9 7.0 %shard_map.67 = (bf16[128,896]{1,0:T(8,128)(2,1)}, bf16[128,896]{1,0:T(8,128)(2,1)}, bf16[128,896]{1,0:T(8,128)(2,1)}, bf16[128,896]{1,0:T(8,128)(2,1)}, bf16[128,896]{1,0:T(8,128)(2,1)}) custom-call(s32[8]{0:T(128)} %iota.70.blocks, bf16[8,2,240,256]{3,2,1,0:T(8,128)(2,1)} %bitcast.42, bf16[2,2048,896]{2,1,0:T(8,128)(2,1)} %refs_8_.1, ...), custom_call_target="tpu_custom_call" | custom-call | flops 1871708160 | bytes 10452992 | tf_op jit(solution)/shard_map/pallas_call | solution.py:176
  285.6 5.1 %collective-permute-start.23 = (bf16[128,896]{1,0:T(8,128)(2,1)}, bf16[128,896]{1,0:T(8,128)(2,1)S(1)}, u32[]{:S(2)}, u32[]{:S(2)}) collective-permute-start(bf16[128,896]{1,0:T(8,128)(2,1)} %get-tuple-element.45), channel_id=1, source_target_pairs={{0,8},{1,9},{2,10},{3,11},{4,12},{5,13},{6,14},{7,15},{8,0},{9,1},... | collective-permute-start | bytes 688136 | tf_op jit(solution)/shard_map/ppermute | solution.py:37
  293.2 4.6 %collective-permute-done.22 = bf16[128,896]{1,0:T(8,128)(2,1)S(1)} collective-permute-done((bf16[128,896]{1,0:T(8,128)(2,1)}, bf16[128,896]{1,0:T(8,128)(2,1)S(1)}, u32[]{:S(2)}, u32[]{:S(2)}) %collective-permute-start.22) | collective-permute-done | bytes 229408 | tf_op jit(solution)/shard_map/ppermute | solution.py:37
  297.8 4.5 %collective-permute-done.23 = bf16[128,896]{1,0:T(8,128)(2,1)S(1)} collective-permute-done((bf16[128,896]{1,0:T(8,128)(2,1)}, bf16[128,896]{1,0:T(8,128)(2,1)S(1)}, u32[]{:S(2)}, u32[]{:S(2)}) %collective-permute-start.23) | collective-permute-done | bytes 229408 | tf_op jit(solution)/shard_map/ppermute | solution.py:37
  302.3 6.9 %collective-permute-done.24 = bf16[128,896]{1,0:T(8,128)(2,1)S(1)} collective-permute-done((bf16[128,896]{1,0:T(8,128)(2,1)}, bf16[128,896]{1,0:T(8,128)(2,1)S(1)}, u32[]{:S(2)}, u32[]{:S(2)}) %collective-permute-start.24) | collective-permute-done | bytes 229408 | tf_op jit(solution)/shard_map/ppermute | solution.py:37
  (237 shorter events, 76.1 us)
Async XLA Ops:
  6.5 250.2 %all-gather.5.cloned.1.call-start = ((), (), s32[]{:S(2)}) async-start(), calls=%async_computation | async-start | bytes 2211840 | tf_op jit(solution)/shard_map/all_gather | solution.py:264
  10.1 24.2 %collective-permute-start = (bf16[1,128,1920]{2,1,0:T(8,128)(2,1)S(1)}, bf16[1,128,1920]{2,1,0:T(8,128)(2,1)S(1)}, u32[]{:S(2)}, u32[]{:S(2)}) collective-permute-start(bf16[1,128,1920]{2,1,0:T(8,128)(2,1)S(1)} %fusion.4.refs_0_), channel_id=1, source_target_pairs={{0,12},{1,13},{2,14},{3,15},{4,0},{5,1},{6,2},{7,3},{8,4},{9,5},{1... | collective-permute-start | bytes 1474568 | tf_op jit(solution)/shard_map/ppermute | solution.py:37
  17.3 24.6 %collective-permute-start.2 = (bf16[1,128,1920]{2,1,0:T(8,128)(2,1)S(1)}, bf16[1,128,1920]{2,1,0:T(8,128)(2,1)S(1)}, u32[]{:S(2)}, u32[]{:S(2)}) collective-permute-start(bf16[1,128,1920]{2,1,0:T(8,128)(2,1)S(1)} %fusion.4.refs_0_), channel_id=1, source_target_pairs={{0,8},{1,9},{2,10},{3,11},{4,12},{5,13},{6,14},{7,15},{8,0},{9,1},... | collective-permute-start | bytes 1474568 | tf_op jit(solution)/shard_map/ppermute | solution.py:37
  17.9 29.7 %collective-permute-start.4 = (bf16[1,128,1920]{2,1,0:T(8,128)(2,1)S(1)}, bf16[1,128,1920]{2,1,0:T(8,128)(2,1)S(1)}, u32[]{:S(2)}, u32[]{:S(2)}) collective-permute-start(bf16[1,128,1920]{2,1,0:T(8,128)(2,1)S(1)} %fusion.4.refs_0_), channel_id=1, source_target_pairs={{0,4},{1,5},{2,6},{3,7},{4,8},{5,9},{6,10},{7,11},{8,12},{9,13},{1... | collective-permute-start | bytes 1474568 | tf_op jit(solution)/shard_map/ppermute | solution.py:37
  38.5 98.3 %collective-permute-start.10 = (bf16[2,3584,256]{2,1,0:T(8,128)(2,1)}, bf16[2,3584,256]{2,1,0:T(8,128)(2,1)}, u32[]{:S(2)}, u32[]{:S(2)}) collective-permute-start(bf16[2,3584,256]{2,1,0:T(8,128)(2,1)} %constant_dynamic-slice_fusion.1), channel_id=1, source_target_pairs={{0,16},{1,17},{2,18},{3,19},{4,20},{5,21},{6,22},{7,23},{8,24},{9,... | collective-permute-start | bytes 11010056 | tf_op jit(solution)/shard_map/ppermute | solution.py:37
  40.6 96.3 %collective-permute-start.11 = (bf16[2,3584,256]{2,1,0:T(8,128)(2,1)}, bf16[2,3584,256]{2,1,0:T(8,128)(2,1)}, u32[]{:S(2)}, u32[]{:S(2)}) collective-permute-start(bf16[2,3584,256]{2,1,0:T(8,128)(2,1)} %constant_dynamic-slice_fusion), channel_id=1, source_target_pairs={{0,16},{1,17},{2,18},{3,19},{4,20},{5,21},{6,22},{7,23},{8,24},{9,... | collective-permute-start | bytes 11010056 | tf_op jit(solution)/shard_map/ppermute | solution.py:37
  43.5 40.9 %collective-permute-start.3 = (bf16[2,128,1920]{2,1,0:T(8,128)(2,1)}, bf16[2,128,1920]{2,1,0:T(8,128)(2,1)S(1)}, u32[]{:S(2)}, u32[]{:S(2)}) collective-permute-start(bf16[2,128,1920]{2,1,0:T(8,128)(2,1)} %constant_dynamic-update-slice_fusion), channel_id=1, source_target_pairs={{0,3},{1,0},{2,1},{3,2},{4,7},{5,4},{6,5},{7,6},{8,11},{9,8},{10,9... | collective-permute-start | bytes 2949128 | tf_op jit(solution)/shard_map/ppermute | solution.py:37
  48.7 47.5 %collective-permute-start.5 = (bf16[2,128,1920]{2,1,0:T(8,128)(2,1)}, bf16[2,128,1920]{2,1,0:T(8,128)(2,1)}, u32[]{:S(2)}, u32[]{:S(2)}) collective-permute-start(bf16[2,128,1920]{2,1,0:T(8,128)(2,1)} %pad_maximum_fusion), channel_id=1, source_target_pairs={{0,1},{1,2},{2,3},{3,0},{4,5},{5,6},{6,7},{7,4},{8,9},{9,10},{10,1... | collective-permute-start | bytes 2949128 | tf_op jit(solution)/shard_map/ppermute | solution.py:37
  48.7 34.6 %collective-permute-start.8 = (bf16[1,128,1792]{2,1,0:T(8,128)(2,1)S(1)}, bf16[1,128,1792]{2,1,0:T(8,128)(2,1)S(1)}, u32[]{:S(2)}, u32[]{:S(2)}) collective-permute-start(bf16[1,128,1792]{2,1,0:T(8,128)(2,1)S(1)} %get-tuple-element.61.refs_5_), channel_id=1, source_target_pairs={{0,1},{1,2},{2,3},{3,0},{4,5},{5,6},{6,7},{7,4},{8,9},{9,10},{10,1... | collective-permute-start | bytes 1376264 | tf_op jit(solution)/shard_map/ppermute | solution.py:37
  84.4 29.6 %collective-permute-start.17 = (bf16[2,128,1920]{2,1,0:T(8,128)(2,1)S(1)}, bf16[2,128,1920]{2,1,0:T(8,128)(2,1)S(1)}, u32[]{:S(2)}, u32[]{:S(2)}) collective-permute-start(bf16[2,128,1920]{2,1,0:T(8,128)(2,1)S(1)} %collective-permute-done.3.refs_1_.refs_3_), channel_id=1, source_target_pairs={{0,3},{1,0},{2,1},{3,2},{4,7},{5,4},{6,5},{7,6},{8,11},{9,8},{10,9... | collective-permute-start | bytes 2949128 | tf_op jit(solution)/shard_map/ppermute | solution.py:37
  96.2 35.2 %collective-permute-start.9 = (bf16[2,128,1792]{2,1,0:T(8,128)(2,1)}, bf16[2,128,1792]{2,1,0:T(8,128)(2,1)}, u32[]{:S(2)}, u32[]{:S(2)}) collective-permute-start(bf16[2,128,1792]{2,1,0:T(8,128)(2,1)} %pad_maximum_fusion.1), channel_id=1, source_target_pairs={{0,4},{1,5},{2,6},{3,7},{4,8},{5,9},{6,10},{7,11},{8,12},{9,13},{1... | collective-permute-start | bytes 2752520 | tf_op jit(solution)/shard_map/ppermute | solution.py:37
  96.2 23.5 %collective-permute-start.18 = (bf16[2,128,1920]{2,1,0:T(8,128)(2,1)}, bf16[2,128,1920]{2,1,0:T(8,128)(2,1)S(1)}, u32[]{:S(2)}, u32[]{:S(2)}) collective-permute-start(bf16[2,128,1920]{2,1,0:T(8,128)(2,1)} %collective-permute-done.5.refs_2_.refs_3_), channel_id=1, source_target_pairs={{0,1},{1,2},{2,3},{3,0},{4,5},{5,6},{6,7},{7,4},{8,9},{9,10},{10,1... | collective-permute-start | bytes 2949128 | tf_op jit(solution)/shard_map/ppermute | solution.py:37
  114.1 22.7 %collective-permute-start.7 = (bf16[2,128,1792]{2,1,0:T(8,128)(2,1)}, bf16[2,128,1792]{2,1,0:T(8,128)(2,1)}, u32[]{:S(2)}, u32[]{:S(2)}) collective-permute-start(bf16[2,128,1792]{2,1,0:T(8,128)(2,1)} %copy-done.22), channel_id=1, source_target_pairs={{0,12},{1,13},{2,14},{3,15},{4,0},{5,1},{6,2},{7,3},{8,4},{9,5},{1... | collective-permute-start | bytes 2752520 | tf_op jit(solution)/shard_map/ppermute | solution.py:37
  153.0 124.4 %all-gather.7.cloned.1.call-start = ((), (), s32[]{:S(2)}) async-start(), calls=%async_computation.1 | async-start | bytes 2211840 | tf_op jit(solution)/shard_map/all_gather | solution.py:264
  153.1 26.0 %collective-permute-start.28 = (bf16[2,128,1920]{2,1,0:T(8,128)(2,1)}, bf16[2,128,1920]{2,1,0:T(8,128)(2,1)S(1)}, u32[]{:S(2)}, u32[]{:S(2)}) collective-permute-start(bf16[2,128,1920]{2,1,0:T(8,128)(2,1)} %constant_dynamic-update-slice_fusion), channel_id=1, source_target_pairs={{0,1},{1,2},{2,3},{3,0},{4,5},{5,6},{6,7},{7,4},{8,9},{9,10},{10,1... | collective-permute-start | bytes 2949128 | tf_op jit(solution)/shard_map/ppermute | solution.py:37
  156.7 24.3 %collective-permute-start.20 = (bf16[2,128,1792]{2,1,0:T(8,128)(2,1)}, bf16[2,128,1792]{2,1,0:T(8,128)(2,1)S(1)}, u32[]{:S(2)}, u32[]{:S(2)}) collective-permute-start(bf16[2,128,1792]{2,1,0:T(8,128)(2,1)} %collective-permute-done.9.refs_7_.refs_9_), channel_id=1, source_target_pairs={{0,4},{1,5},{2,6},{3,7},{4,8},{5,9},{6,10},{7,11},{8,12},{9,13},{1... | collective-permute-start | bytes 2752520 | tf_op jit(solution)/shard_map/ppermute | solution.py:37
  156.7 24.8 %collective-permute-start.19 = (bf16[2,128,1792]{2,1,0:T(8,128)(2,1)}, bf16[2,128,1792]{2,1,0:T(8,128)(2,1)}, u32[]{:S(2)}, u32[]{:S(2)}) collective-permute-start(bf16[2,128,1792]{2,1,0:T(8,128)(2,1)} %collective-permute-done.7.refs_6_.refs_9_), channel_id=1, source_target_pairs={{0,12},{1,13},{2,14},{3,15},{4,0},{5,1},{6,2},{7,3},{8,4},{9,5},{1... | collective-permute-start | bytes 2752520 | tf_op jit(solution)/shard_map/ppermute | solution.py:37
  160.4 33.3 %collective-permute-start.27 = (bf16[2,128,1920]{2,1,0:T(8,128)(2,1)}, bf16[2,128,1920]{2,1,0:T(8,128)(2,1)S(1)}, u32[]{:S(2)}, u32[]{:S(2)}) collective-permute-start(bf16[2,128,1920]{2,1,0:T(8,128)(2,1)} %pad_maximum_fusion), channel_id=1, source_target_pairs={{0,3},{1,0},{2,1},{3,2},{4,7},{5,4},{6,5},{7,6},{8,11},{9,8},{10,9... | collective-permute-start | bytes 2949128 | tf_op jit(solution)/shard_map/ppermute | solution.py:37
  160.7 39.3 %collective-permute-start.30 = (bf16[2,128,1792]{2,1,0:T(8,128)(2,1)}, bf16[2,128,1792]{2,1,0:T(8,128)(2,1)}, u32[]{:S(2)}, u32[]{:S(2)}) collective-permute-start(bf16[2,128,1792]{2,1,0:T(8,128)(2,1)} %pad_maximum_fusion.1), channel_id=1, source_target_pairs={{0,12},{1,13},{2,14},{3,15},{4,0},{5,1},{6,2},{7,3},{8,4},{9,5},{1... | collective-permute-start | bytes 2752520 | tf_op jit(solution)/shard_map/ppermute | solution.py:37
  179.1 24.3 %collective-permute-start.29 = (bf16[2,128,1792]{2,1,0:T(8,128)(2,1)}, bf16[2,128,1792]{2,1,0:T(8,128)(2,1)}, u32[]{:S(2)}, u32[]{:S(2)}) collective-permute-start(bf16[2,128,1792]{2,1,0:T(8,128)(2,1)} %copy-done.22), channel_id=1, source_target_pairs={{0,4},{1,5},{2,6},{3,7},{4,8},{5,9},{6,10},{7,11},{8,12},{9,13},{1... | collective-permute-start | bytes 2752520 | tf_op jit(solution)/shard_map/ppermute | solution.py:37
  251.1 17.2 %collective-permute-start.41 = (bf16[128,896]{1,0:T(8,128)(2,1)}, bf16[128,896]{1,0:T(8,128)(2,1)S(1)}, u32[]{:S(2)}, u32[]{:S(2)}) collective-permute-start(bf16[128,896]{1,0:T(8,128)(2,1)} %get-tuple-element.53), channel_id=1, source_target_pairs={{0,7},{1,4},{2,5},{3,6},{4,11},{5,8},{6,9},{7,10},{8,15},{9,12},{1... | collective-permute-start | bytes 688136 | tf_op jit(solution)/shard_map/ppermute | solution.py:37
  253.0 21.9 %collective-permute-start.42 = (bf16[128,896]{1,0:T(8,128)(2,1)}, bf16[128,896]{1,0:T(8,128)(2,1)S(1)}, u32[]{:S(2)}, u32[]{:S(2)}) collective-permute-start(bf16[128,896]{1,0:T(8,128)(2,1)} %get-tuple-element.54), channel_id=1, source_target_pairs={{0,14},{1,15},{2,12},{3,13},{4,2},{5,3},{6,0},{7,1},{8,6},{9,7},{1... | collective-permute-start | bytes 688136 | tf_op jit(solution)/shard_map/ppermute | solution.py:37
  255.6 19.6 %collective-permute-start.43 = (bf16[128,896]{1,0:T(8,128)(2,1)}, bf16[128,896]{1,0:T(8,128)(2,1)S(1)}, u32[]{:S(2)}, u32[]{:S(2)}) collective-permute-start(bf16[128,896]{1,0:T(8,128)(2,1)} %get-tuple-element.55), channel_id=1, source_target_pairs={{0,1},{1,2},{2,3},{3,0},{4,5},{5,6},{6,7},{7,4},{8,9},{9,10},{10,1... | collective-permute-start | bytes 688136 | tf_op jit(solution)/shard_map/ppermute | solution.py:37
  264.3 20.6 %collective-permute-start.44 = (bf16[128,896]{1,0:T(8,128)(2,1)S(1)}, bf16[128,896]{1,0:T(8,128)(2,1)S(1)}, u32[]{:S(2)}, u32[]{:S(2)}) collective-permute-start(bf16[128,896]{1,0:T(8,128)(2,1)S(1)} %copy-done.29), channel_id=1, source_target_pairs={{0,4},{1,5},{2,6},{3,7},{4,8},{5,9},{6,10},{7,11},{8,12},{9,13},{1... | collective-permute-start | bytes 688136 | tf_op jit(solution)/shard_map/ppermute | solution.py:37
  265.6 20.0 %collective-permute-start.13 = (bf16[128,896]{1,0:T(8,128)(2,1)}, bf16[128,896]{1,0:T(8,128)(2,1)S(1)}, u32[]{:S(2)}, u32[]{:S(2)}) collective-permute-start(bf16[128,896]{1,0:T(8,128)(2,1)} %get-tuple-element.38), channel_id=1, source_target_pairs={{0,5},{1,6},{2,7},{3,4},{4,9},{5,10},{6,11},{7,8},{8,13},{9,14},{1... | collective-permute-start | bytes 688136 | tf_op jit(solution)/shard_map/ppermute | solution.py:37
  268.4 22.3 %collective-permute-start.14 = (bf16[128,896]{1,0:T(8,128)(2,1)}, bf16[128,896]{1,0:T(8,128)(2,1)S(1)}, u32[]{:S(2)}, u32[]{:S(2)}) collective-permute-start(bf16[128,896]{1,0:T(8,128)(2,1)} %get-tuple-element.39), channel_id=1, source_target_pairs={{0,15},{1,12},{2,13},{3,14},{4,3},{5,0},{6,1},{7,2},{8,7},{9,4},{1... | collective-permute-start | bytes 688136 | tf_op jit(solution)/shard_map/ppermute | solution.py:37
  274.9 16.5 %collective-permute-start.15 = (bf16[128,896]{1,0:T(8,128)(2,1)}, bf16[128,896]{1,0:T(8,128)(2,1)S(1)}, u32[]{:S(2)}, u32[]{:S(2)}) collective-permute-start(bf16[128,896]{1,0:T(8,128)(2,1)} %get-tuple-element.40), channel_id=1, source_target_pairs={{0,3},{1,0},{2,1},{3,2},{4,7},{5,4},{6,5},{7,6},{8,11},{9,8},{10,9... | collective-permute-start | bytes 688136 | tf_op jit(solution)/shard_map/ppermute | solution.py:37
  275.2 16.4 %collective-permute-start.16 = (bf16[128,896]{1,0:T(8,128)(2,1)}, bf16[128,896]{1,0:T(8,128)(2,1)S(1)}, u32[]{:S(2)}, u32[]{:S(2)}) collective-permute-start(bf16[128,896]{1,0:T(8,128)(2,1)} %get-tuple-element.41), channel_id=1, source_target_pairs={{0,12},{1,13},{2,14},{3,15},{4,0},{5,1},{6,2},{7,3},{8,4},{9,5},{1... | collective-permute-start | bytes 688136 | tf_op jit(solution)/shard_map/ppermute | solution.py:37
  285.6 16.8 %collective-permute-start.23 = (bf16[128,896]{1,0:T(8,128)(2,1)}, bf16[128,896]{1,0:T(8,128)(2,1)S(1)}, u32[]{:S(2)}, u32[]{:S(2)}) collective-permute-start(bf16[128,896]{1,0:T(8,128)(2,1)} %get-tuple-element.45), channel_id=1, source_target_pairs={{0,8},{1,9},{2,10},{3,11},{4,12},{5,13},{6,14},{7,15},{8,0},{9,1},... | collective-permute-start | bytes 688136 | tf_op jit(solution)/shard_map/ppermute | solution.py:37
  290.7 18.6 %collective-permute-start.24 = (bf16[128,896]{1,0:T(8,128)(2,1)}, bf16[128,896]{1,0:T(8,128)(2,1)S(1)}, u32[]{:S(2)}, u32[]{:S(2)}) collective-permute-start(bf16[128,896]{1,0:T(8,128)(2,1)} %get-tuple-element.46), channel_id=1, source_target_pairs={{0,2},{1,3},{2,0},{3,1},{4,6},{5,7},{6,4},{7,5},{8,10},{9,11},{10,... | collective-permute-start | bytes 688136 | tf_op jit(solution)/shard_map/ppermute | solution.py:37
  291.4 17.8 %collective-permute-start.25 = (bf16[128,896]{1,0:T(8,128)(2,1)}, bf16[128,896]{1,0:T(8,128)(2,1)S(1)}, u32[]{:S(2)}, u32[]{:S(2)}) collective-permute-start(bf16[128,896]{1,0:T(8,128)(2,1)} %get-tuple-element.47), channel_id=1, source_target_pairs={{0,9},{1,10},{2,11},{3,8},{4,13},{5,14},{6,15},{7,12},{8,1},{9,2},... | collective-permute-start | bytes 688136 | tf_op jit(solution)/shard_map/ppermute | solution.py:37
  291.7 18.5 %collective-permute-start.26 = (bf16[128,896]{1,0:T(8,128)(2,1)}, bf16[128,896]{1,0:T(8,128)(2,1)S(1)}, u32[]{:S(2)}, u32[]{:S(2)}) collective-permute-start(bf16[128,896]{1,0:T(8,128)(2,1)} %get-tuple-element.48), channel_id=1, source_target_pairs={{0,6},{1,7},{2,4},{3,5},{4,10},{5,11},{6,8},{7,9},{8,14},{9,15},{1... | collective-permute-start | bytes 688136 | tf_op jit(solution)/shard_map/ppermute | solution.py:37
  (47 other events, 810.3 us)
Sparse Core Ops, SparseCore 0:
  153.1 27.4 all-gather.4
  198.2 25.5 all-gather.6
